TPU v7x, 512 devices: a whole 4x8x8 slice. The times are simulated.
512 devices in a mesh: row: 16 (over x, y_hi, core), col: 32 (over y_lo, z).
Axes of the slice: x: 4, y: 8 (y_hi: 2, y_lo: 4; y = y_hi * 4 + y_lo), z: 8, core: 2. Of those that a mesh axis runs over, the one named last changes fastest.
Arguments:
- vectors: bfloat16 [16, 524288], P(None, ('row', 'col')), may hold values from -6 to 6
- tiles: bfloat16 [16, 32, 8, 512, 512], P('row', 'col'), may hold values from -0.25 to 0.25
- block_rows: int32 [16, 32, 8], P('row', 'col'), may hold values from 0 to 63
- block_cols: int32 [16, 32, 8], P('row', 'col'), may hold values from 0 to 31
- counts: int32 [16, 32], P('row', 'col'), may hold values from 1 to 8, as said below
Outputs:
- hx: float32 [16, 524288], P(None, ('row', 'col'))
Inputs may be any that keep to these rules, and one draw needn't show every extreme that they name: `counts`: every tile has between 1 and 8 live blocks; in every draw one tile has all 8 slots live, the others at most half.
All inputs are finite; a program needn't handle non-finite values.
Results may differ from a plain program's by a relative error of at most 0.0003.
Values may be sent and summed in bfloat16 or wider, within the bound.
A program may use at most 64 MiB of HBM per device.

v0:
```python
import jax
import jax.numpy as jnp
from jax import lax
from jax.sharding import PartitionSpec as P


def add_at(total, piece, start):
    width = piece.shape[1]
    old = lax.dynamic_slice_in_dim(total, start, width, 1)
    return lax.dynamic_update_slice_in_dim(total, old + piece, start, 1)


def sum_over_cols(partial_value):
    return lax.psum_scatter(partial_value, "col", scatter_dimension=1, tiled=True)


def sum_over_rows(partial_value):
    return lax.psum_scatter(partial_value, "row", scatter_dimension=1, tiled=True)


def on_device(vectors, tiles, block_rows, block_cols, counts):
    block_size = tiles.shape[-1]
    local_tiles = tiles[0, 0]
    row_local = block_rows[0, 0]
    col_local = block_cols[0, 0]
    live_count = counts[0, 0]
    row_vectors = lax.all_gather(vectors, "col", axis=1, tiled=True)
    col_vectors = lax.all_gather(vectors, "row", axis=1, tiled=True)
    row_total = jnp.zeros((vectors.shape[0], row_vectors.shape[1]), jnp.float32)
    col_total = jnp.zeros((vectors.shape[0], col_vectors.shape[1]), jnp.float32)

    def both_add(slot_index, totals):
        block = lax.dynamic_index_in_dim(local_tiles, slot_index, 0, keepdims=False)
        row_start = row_local[slot_index] * block_size
        col_start = col_local[slot_index] * block_size
        col_piece = lax.dynamic_slice_in_dim(col_vectors, col_start, block_size, 1)
        row_piece = lax.dynamic_slice_in_dim(row_vectors, row_start, block_size, 1)
        direct = lax.dot_general(
            col_piece, block, (((1,), (1,)), ((), ())), preferred_element_type=jnp.float32
        )
        mirror = jnp.dot(row_piece, block, preferred_element_type=jnp.float32)
        return (add_at(totals[0], direct, row_start), add_at(totals[1], mirror, col_start))

    totals = lax.fori_loop(0, live_count, both_add, (row_total, col_total))
    row_result = sum_over_cols(totals[0])
    col_result = sum_over_rows(totals[1])
    return row_result + col_result


def solution(mesh):
    placed = (
        P(None, ("row", "col")),
        P("row", "col", None, None, None),
        P("row", "col", None),
        P("row", "col", None),
        P("row", "col"),
    )
    return jax.shard_map(
        on_device, mesh=mesh, in_specs=placed, out_specs=P(None, ("row", "col")), check_vma=False
    )
```

profile of v0, /device:TPU:4, one launch (start us, length us, event | category | flops | bytes accessed | tf_op | source)
XLA Modules:
  0.0 463.6 jit_solution(15266301294986820063)
XLA Ops:
  6.5 0.0 copy-start.3
  6.5 0.0 copy-start.2
  6.5 0.0 all-gather.2.cloned.1.call-start
  6.5 0.7 all-gather.2.cloned.1.call-update
  7.3 0.0 reduce-scatter.5.cloned.1.call-start
  7.3 33.5 %all_gather.6 = bf16[16,16384]{1,0:T(8,128)(2,1)} all-gather(bf16[16,1024]{1,0:T(8,128)(2,1)} %param.7), channel_id=1, replica_groups=mesh['row'=16,'col'=32] {'row'}, dimensions={1}, use_global_device_ids=true | all-gather | bytes 557056 | tf_op jit(solution)/shard_map/all_gather | solution.py:28
  40.8 127.2 %all-gather.2.cloned.1.call-done = bf16[16,32768]{1,0:T(8,128)(2,1)} async-done(((bf16[16,1024]{1,0:T(8,128)(2,1)}), bf16[16,32768]{1,0:T(8,128)(2,1)}) %all-gather.2.cloned.1.call-update) | async-done | bytes 1048592 | tf_op jit(solution)/shard_map/all_gather | solution.py:27
  168.0 0.1 broadcast_in_dim.7
  168.1 0.1 broadcast_in_dim.6
  168.2 0.0 copy-done.3
  168.3 0.0 copy-done.2
  168.3 6.6 %while.12 = (s32[]{:T(128)}, f32[16,32768]{1,0:T(8,128)S(1)}, f32[16,16384]{1,0:T(8,128)S(1)}, s32[]{:T(128)}, s32[8]{0:T(128)S(1)}, /*index=5*/s32[8]{0:T(128)S...) while((s32[]{:T(128)}, f32[16,32768]{1,0:T(8,128)S(1)}, ...), condition=%wide.region_1.2_spmd, body=%wide.region_0.1_spmd.sunk | while | flops 16793612 | bytes 1212739 | solution.py:44
  168.9 0.7 dynamic_slice.50
  170.3 0.7 dynamic_slice.51
  171.6 1.2 fusion.21
  172.9 1.3 fusion.20
  174.8 0.0 copy-start.1
  174.8 0.0 copy-start
  174.9 1.0 copy-done.1
  175.8 0.0 reduce-scatter.5.cloned.1.call-update
  175.8 0.0 reduce-scatter.3.cloned.1.call-start
  175.9 0.6 copy-done
  176.5 0.1 reduce-scatter.3.cloned.1.call-update
  176.6 113.0 %reduce-scatter.5.cloned.1.call-done = f32[16,1024]{1,0:T(8,128)} async-done(((f32[16,16384]{1,0:T(8,128)}), f32[16,1024]{1,0:T(8,128)}) %reduce-scatter.5.cloned.1.call-update) | async-done | bytes 65552 | tf_op jit(solution)/shard_map/reduce_scatter | solution.py:18
  289.6 166.0 %reduce-scatter.3.cloned.1.call-done = f32[16,1024]{1,0:T(8,128)} async-done(((f32[16,32768]{1,0:T(8,128)}), f32[16,1024]{1,0:T(8,128)}) %reduce-scatter.3.cloned.1.call-update) | async-done | bytes 65552 | tf_op jit(solution)/shard_map/reduce_scatter | solution.py:14
  455.6 1.5 add.32
Async XLA Ops:
  6.5 161.7 %copy-start.3 = (s32[1,1,8]{2,1,0:T(1,128)S(1)}, s32[1,1,8]{2,1,0:T(1,128)}, u32[]{:S(2)}) copy-start(s32[1,1,8]{2,1,0:T(1,128)} %param.10) | copy-start | bytes 100
  6.5 161.7 %copy-start.2 = (s32[1,1,8]{2,1,0:T(1,128)S(1)}, s32[1,1,8]{2,1,0:T(1,128)}, u32[]{:S(2)}) copy-start(s32[1,1,8]{2,1,0:T(1,128)} %param.9) | copy-start | bytes 100
  6.5 161.5 %all-gather.2.cloned.1.call-start = ((), (), s32[]{:S(2)}) async-start(), calls=%async_computation.2 | async-start | bytes 1081344 | tf_op jit(solution)/shard_map/all_gather | solution.py:27
  7.3 282.3 %reduce-scatter.5.cloned.1.call-start = ((), (), s32[]{:S(2)}) async-start(), calls=%async_computation.4 | async-start | bytes 1114112 | tf_op jit(solution)/shard_map/reduce_scatter | solution.py:18
  174.8 1.0 copy-start.1
  174.8 1.6 copy-start
  175.8 279.7 %reduce-scatter.3.cloned.1.call-start = ((), (), s32[]{:S(2)}) async-start(), calls=%async_computation.3 | async-start | bytes 2162688 | tf_op jit(solution)/shard_map/reduce_scatter | solution.py:14
Sparse Core Ops, SparseCore 0:
  9.4 158.5 all-gather.1
  176.0 113.5 reduce-scatter.4
  292.6 162.9 reduce-scatter.2
where the time goes:
time: 457 us; the launch traced here: 464 us
  waiting for transfers between devices  407 us (89%)
  blocking collectives  33.5 us (7%)
  between operations  13.2 us (3%)
    reduce_scatter x1, waiting for transfers between devices, sum_over_cols(): lax.psum_scatter(partial_value, 'col', scatter_dimension=1, tiled=True)  166 us
    all_gather x1, waiting for transfers between devices, on_device(): row_vectors = lax.all_gather(vectors, 'col', axis=1, tiled=True)  127 us
    reduce_scatter x1, waiting for transfers between devices, sum_over_rows(): lax.psum_scatter(partial_value, 'row', scatter_dimension=1, tiled=True)  113 us
    all_gather x1, blocking collectives, on_device(): col_vectors = lax.all_gather(vectors, 'row', axis=1, tiled=True)  33.5 us
  transfers between devices with their start and end apart: 3, of which 3 were waited for; matrix products, arithmetic and copies ran while one was open for 0% of the time, Pallas kernels for 0%

commit v1 on v0

v1 whole, which is shorter than its diff:
```python
import jax
import jax.numpy as jnp
from jax import lax
from jax.experimental import pallas as pl
from jax.experimental.pallas import tpu as pltpu
from jax.sharding import PartitionSpec as P

NX, NH, NC = 4, 2, 2
NY, NZ = 4, 8
VECS, BLK, SLOTS = 16, 512, 8
LANES = 128
LT = BLK // LANES
EXPO = SLOTS * LT
INDEX = EXPO + 1
MSG = INDEX + 1
MESH = pl.DeviceIdType.MESH
TINY = 2.0 ** -110


def exponent_of(most):
    return jnp.ceil(jnp.log2(jnp.maximum(most, TINY)) - 14.98)


def coded(values, inverse):
    return jnp.round(values * inverse).astype(jnp.int32).astype(jnp.int16)


def decoded(code):
    return code.astype(jnp.int32).astype(jnp.float32)


def most_of(parts):
    most = jnp.abs(parts[0])
    for part in parts[1:]:
        most = jnp.maximum(most, jnp.abs(part))
    return most


def kernel(
    vec, tiles, br, bc, cnt, out,
    rowbuf, colbuf, tilebuf, prod, ymsg, cmsg, dec, idxb, acc,
    zsend, zrecv, xsend, xrecv, hsend, hrecv, own,
    tsem, ys, yr, zs, zr, cs, cr, ss, sr, ms, mr, ks, kr, ps, pr, xs, xr, hs, hr,
):
    me_r, me_c = lax.axis_index("row"), lax.axis_index("col")
    x, h, core = me_r // (NH * NC), (me_r // NC) % NH, me_r % NC
    y, z = me_c // NZ, me_c % NZ

    def row_of(xx, hh, cc):
        return (xx * NH + hh) * NC + cc

    def col_of(yy, zz):
        return yy * NZ + zz

    def y_at(d):
        return (y + d + NY) % NY

    def z_at(d):
        return (z + d + NZ) % NZ

    def x_at(d):
        return (x + d + NX) % NX

    sibling = (row_of(x, h, 1 - core), me_c)
    far = (row_of(x, 1 - h, core), me_c)
    x_peer = [None] + [(row_of(x_at(d), h, core), me_c) for d in range(1, NX)]
    y_peer = [None] + [(me_r, col_of(y_at(d), z)) for d in range(1, NY)]
    z_peer = [None] + [(me_r, col_of(y, z_at(d))) for d in range(1, NZ)]

    def remote(src, dst, send, recv, device):
        return pltpu.make_async_remote_copy(
            src_ref=src, dst_ref=dst, send_sem=send, recv_sem=recv,
            device_id=device, device_id_type=MESH,
        )

    sent = []

    def send(*args):
        copy = remote(*args)
        copy.start()
        sent.append(copy)

    for s in range(SLOTS):
        pltpu.make_async_copy(tiles.at[s], tilebuf.at[s], tsem.at[s]).start()
    for k in range(2):
        piece = vec[:, k * BLK:(k + 1) * BLK]
        rowbuf[2 * me_c + k] = piece
        colbuf[2 * me_r + k] = piece

    barrier = pltpu.get_barrier_semaphore()
    partners = [sibling, far] + x_peer[1:] + y_peer[1:] + z_peer[1:]
    for device in partners:
        pl.semaphore_signal(barrier, inc=1, device_id=device, device_id_type=MESH)
    pl.semaphore_wait(barrier, len(partners))

    def row_chunk(dy, dz):
        return rowbuf.at[pl.ds(2 * col_of(y_at(-dy), z_at(-dz)), 2)]

    def col_chunk(d, e, cc):
        return colbuf.at[pl.ds(2 * row_of(x_at(-d), (h + e) % NH, cc), 2)]

    def relay(way, hop, i):
        chunk = row_chunk(i, way * hop)
        w = 0 if way > 0 else 1
        send(chunk, chunk, zs.at[w, hop, i], zr.at[w, hop, i], z_peer[way % NZ])

    def relay_wait(way, hop, i):
        chunk = row_chunk(i, way * (hop + 1))
        w = 0 if way > 0 else 1
        remote(chunk, chunk, zs.at[w, hop, i], zr.at[w, hop, i], z_peer[1]).wait_recv()

    def last_goes(way, i):
        return (i < NY // 2) == (way > 0)

    mine_row, mine_col = row_chunk(0, 0), col_chunk(0, 0, core)
    relay(1, 0, 0)
    relay(-1, 0, 0)
    send(mine_col, mine_col, cs.at[0, 1], cr.at[0, 1], far)
    for d in range(1, NY):
        send(mine_row, mine_row, ys.at[d], yr.at[d], y_peer[d])
    for d in range(1, NX):
        send(mine_col, mine_col, cs.at[d, 0], cr.at[d, 0], x_peer[d])
    send(mine_col, mine_col, ss.at[0, 0], sr.at[0, 0], sibling)

    for i in range(1, NY):
        chunk = row_chunk(i, 0)
        remote(chunk, chunk, ys.at[i], yr.at[i], y_peer[1]).wait_recv()
        relay(1, 0, i)
        relay(-1, 0, i)

    def col_wait(d, e):
        chunk = col_chunk(d, e, core)
        remote(chunk, chunk, cs.at[d, e], cr.at[d, e], far).wait_recv()

    col_wait(0, 1)
    theirs = col_chunk(0, 1, core)
    for d in range(1, NX):
        send(theirs, theirs, cs.at[d, 1], cr.at[d, 1], x_peer[d])
    send(theirs, theirs, ss.at[0, 1], sr.at[0, 1], sibling)

    for i in range(NY):
        for way in (1, -1):
            relay_wait(way, 0, i)
            relay(way, 1, i)

    for e in range(NH):
        for d in range(1, NX):
            col_wait(d, e)
            chunk = col_chunk(d, e, core)
            send(chunk, chunk, ss.at[d, e], sr.at[d, e], sibling)

    for i in range(NY):
        for way in (1, -1):
            relay_wait(way, 1, i)
            relay(way, 2, i)

    for e in range(NH):
        for d in range(NX):
            chunk = col_chunk(d, e, 1 - core)
            remote(chunk, chunk, ss.at[d, e], sr.at[d, e], sibling).wait_recv()

    live = cnt[0]
    lane_row = lax.broadcasted_iota(jnp.int32, (VECS, LANES), 0)

    def lane_parts(value):
        return [value[:, j * LANES:(j + 1) * LANES] for j in range(LT)]

    def products(pieces, where, to, contract, wait, msg):
        def one(s, most):
            if wait:
                pltpu.make_async_copy(tiles.at[s], tilebuf.at[s], tsem.at[s]).wait()
            value = lax.dot_general(
                pieces[where[s]], tilebuf[s], (((1,), (contract,)), ((), ())),
                preferred_element_type=jnp.float32,
            )
            value = jnp.where(s < live, value, 0.0)
            prod[s] = value
            return jnp.maximum(most, most_of(lane_parts(value)))

        most = lax.fori_loop(0, SLOTS, one, jnp.zeros((VECS, LANES), jnp.float32))
        exponent = exponent_of(most)
        inverse = 1.0 / jnp.exp2(exponent)

        def code(s, carry):
            for j, part in enumerate(lane_parts(prod[s])):
                msg[0, s * LT + j] = coded(part, inverse)
            return carry

        lax.fori_loop(0, SLOTS, code, 0)
        msg[0, EXPO] = exponent.astype(jnp.int32).astype(jnp.int16)
        index = jnp.full((VECS, LANES), -1, jnp.int32)
        for s in range(SLOTS):
            index = jnp.where(lane_row == s, jnp.where(s < live, to[s], -1), index)
        msg[0, INDEX] = index.astype(jnp.int16)

    def combine(msg, sources, target_of):
        for n in range(sources):
            scale = jnp.exp2(decoded(msg[n, EXPO]))
            index = msg[n, INDEX].astype(jnp.int32)
            for s in range(SLOTS):
                idxb[n * SLOTS + s] = jnp.broadcast_to(index[s:s + 1], (VECS, LANES))

            def open_slot(t, carry):
                dec[n * SLOTS * LT + t] = decoded(msg[n, t]) * scale
                return carry

            lax.fori_loop(0, SLOTS * LT, open_slot, 0)

        def lane_tile(j, carry):
            def candidate(c, sums):
                value, index = dec[c * LT + j], idxb[c]
                return tuple(
                    total + jnp.where(index == target_of(t), value, 0.0)
                    for t, total in enumerate(sums)
                )

            zero = jnp.zeros((VECS, LANES), jnp.float32)
            sums = lax.fori_loop(0, sources * SLOTS, candidate, (zero,) * 16)
            for t in range(16):
                acc[t, j] = sums[t]
            return carry

        lax.fori_loop(0, LT, lane_tile, 0)

    products(colbuf, bc, br, 1, True, ymsg)
    for d in range(1, NY):
        send(ymsg.at[0], ymsg.at[d], ps.at[d], pr.at[d], y_peer[d])

    for i in range(NY):
        for way in (1, -1):
            relay_wait(way, 2, i)
            if last_goes(way, i):
                relay(way, 3, i)
    for i in range(NY):
        relay_wait(1 if last_goes(1, i) else -1, 3, i)

    products(rowbuf, br, bc, 0, False, cmsg)
    send(cmsg.at[0], cmsg.at[1], ms.at[0], mr.at[0], sibling)

    for d in range(1, NY):
        remote(ymsg.at[0], ymsg.at[d], ps.at[d], pr.at[d], y_peer[1]).wait_recv()
    combine(ymsg, NY, lambda t: 2 * col_of(y, 0) + t)

    def code_chunk(parts, dst, first):
        exponent = exponent_of(most_of(parts))
        inverse = 1.0 / jnp.exp2(exponent)
        for t, part in enumerate(parts):
            dst[first + t] = coded(part, inverse)
        dst[first + len(parts)] = exponent.astype(jnp.int32).astype(jnp.int16)

    for d in range(1, NZ):
        to = z_at(d)
        code_chunk([acc[2 * to + k, j] for k in range(2) for j in range(LT)], zsend.at[d], 0)
        send(zsend.at[d], zrecv.at[d], ks.at[d], kr.at[d], z_peer[d])
    for k in range(2):
        for j in range(LT):
            own[k * LT + j] = acc[2 * z + k, j]

    remote(cmsg.at[0], cmsg.at[1], ms.at[0], mr.at[0], sibling).wait_recv()
    combine(cmsg, NC, lambda t: (t // 2) * 2 * NC + 2 * core + t % 2)
    CH = 2 * LT + 1
    for d in range(1, NX):
        for e in range(NH):
            chip = x_at(d) * NH + (h + e) % NH
            code_chunk([acc[2 * chip + k, j] for k in range(2) for j in range(LT)], xsend.at[d], e * CH)
        send(xsend.at[d], xrecv.at[d], xs.at[d], xr.at[d], x_peer[d])
    for d in range(1, NX):
        remote(xsend.at[d], xrecv.at[d], xs.at[d], xr.at[d], x_peer[1]).wait_recv()

    def opened(msg, first):
        scale = jnp.exp2(decoded(msg[first + 2 * LT]))
        return [decoded(msg[first + t]) * scale for t in range(2 * LT)]

    def with_x(e):
        chip = x * NH + (h + e) % NH
        parts = [acc[2 * chip + k, j] for k in range(2) for j in range(LT)]
        for d in range(1, NX):
            parts = [a + b for a, b in zip(parts, opened(xrecv.at[d], e * CH))]
        return parts

    code_chunk(with_x(1), hsend, 0)
    send(hsend, hrecv, hs.at[0], hr.at[0], far)
    total = [a + own[t] for t, a in enumerate(with_x(0))]
    for d in range(1, NZ):
        remote(zsend.at[d], zrecv.at[d], ks.at[d], kr.at[d], z_peer[1]).wait_recv()
        total = [a + b for a, b in zip(total, opened(zrecv.at[d], 0))]
    remote(hsend, hrecv, hs.at[0], hr.at[0], far).wait_recv()
    total = [a + b for a, b in zip(total, opened(hrecv, 0))]
    for t, part in enumerate(total):
        out[:, t * LANES:(t + 1) * LANES] = part

    for copy in sent:
        copy.wait_send()


def on_device(vectors, tiles, block_rows, block_cols, counts):
    i16, f32, bf16 = jnp.int16, jnp.float32, jnp.bfloat16
    chunk = 2 * LT + 1
    dma = pltpu.SemaphoreType.DMA
    scratch = [
        pltpu.VMEM((2 * NY * NZ, VECS, BLK), bf16),
        pltpu.VMEM((2 * NX * NH * NC, VECS, BLK), bf16),
        pltpu.VMEM((SLOTS, BLK, BLK), bf16),
        pltpu.VMEM((SLOTS, VECS, BLK), f32),
        pltpu.VMEM((NY, MSG, VECS, LANES), i16),
        pltpu.VMEM((NC, MSG, VECS, LANES), i16),
        pltpu.VMEM((NY * SLOTS * LT, VECS, LANES), f32),
        pltpu.VMEM((NY * SLOTS, VECS, LANES), jnp.int32),
        pltpu.VMEM((16, LT, VECS, LANES), f32),
        pltpu.VMEM((NZ, chunk, VECS, LANES), i16),
        pltpu.VMEM((NZ, chunk, VECS, LANES), i16),
        pltpu.VMEM((NX, NH * chunk, VECS, LANES), i16),
        pltpu.VMEM((NX, NH * chunk, VECS, LANES), i16),
        pltpu.VMEM((chunk, VECS, LANES), i16),
        pltpu.VMEM((chunk, VECS, LANES), i16),
        pltpu.VMEM((2 * LT, VECS, LANES), f32),
        dma((SLOTS,)),
        dma((NY,)), dma((NY,)),
        dma((2, NZ // 2, NY)), dma((2, NZ // 2, NY)),
        dma((NX, NH)), dma((NX, NH)),
        dma((NX, NH)), dma((NX, NH)),
        dma((1,)), dma((1,)),
        dma((NZ,)), dma((NZ,)),
        dma((NY,)), dma((NY,)),
        dma((NX,)), dma((NX,)),
        dma((1,)), dma((1,)),
    ]
    return pl.pallas_call(
        kernel,
        out_shape=jax.ShapeDtypeStruct((VECS, 2 * BLK), f32),
        in_specs=[
            pl.BlockSpec(memory_space=pltpu.VMEM),
            pl.BlockSpec(memory_space=pl.ANY),
            pl.BlockSpec(memory_space=pltpu.SMEM),
            pl.BlockSpec(memory_space=pltpu.SMEM),
            pl.BlockSpec(memory_space=pltpu.SMEM),
        ],
        out_specs=pl.BlockSpec(memory_space=pltpu.VMEM),
        scratch_shapes=scratch,
        compiler_params=pltpu.CompilerParams(
            collective_id=0, has_side_effects=True, vmem_limit_bytes=40 * 2 ** 20
        ),
    )(
        vectors,
        tiles.reshape(SLOTS, BLK, BLK),
        block_rows.reshape(SLOTS),
        block_cols.reshape(SLOTS),
        counts.reshape(1),
    )


def solution(mesh):
    placed = (
        P(None, ("row", "col")),
        P("row", "col", None, None, None),
        P("row", "col", None),
        P("row", "col", None),
        P("row", "col"),
    )
    return jax.shard_map(
        on_device, mesh=mesh, in_specs=placed, out_specs=P(None, ("row", "col")), check_vma=False
    )
```

time: 457 us -> 65.4 us (0.14)
  the two profiles are of different devices: /device:TPU:4 before, /device:TPU:56 now
where the time goes in v1:
time: 65.4 us; the launch traced here: 65.2 us
  Pallas kernels  59.7 us (91%)
  local copies, waits for them, and re-layouts  4.88 us (7%)
  between operations  0.67 us (1%)
    pallas_call x1, Pallas kernels, on_device(): pl.pallas_call(kernel, out_shape=jax.ShapeDtypeStruct((VECS, 2 * BLK), f3...  59.7 us
    unnamed x9, local copies, waits for them, and re-layouts  4.88 us

profile of v1, /device:TPU:56, one launch (start us, length us, event | category | flops | bytes accessed | tf_op | source)
XLA Modules:
  0.0 65.2 jit_solution(9343357922854095147)
XLA Ops:
  0.7 0.0 copy-start
  0.7 2.2 %copy-done = bf16[1,1,8,512,512]{4,3,2,1,0:T(8,128)(2,1)S(1)} copy-done((bf16[1,1,8,512,512]{4,3,2,1,0:T(8,128)(2,1)S(1)}, bf16[1,1,8,512,512]{4,3,2,1,0:T(8,128)(2,1)}, u32[]{:S(2)}) %copy-start) | copy-done | bytes 4194328
  2.8 0.0 copy-start.1
  2.8 0.8 %copy-done.1 = bf16[16,1024]{1,0:T(8,128)(2,1)S(1)} copy-done((bf16[16,1024]{1,0:T(8,128)(2,1)S(1)}, bf16[16,1024]{1,0:T(8,128)(2,1)}, u32[]{:S(2)}) %copy-start.1) | copy-done | bytes 32792
  3.6 0.0 copy-start.2
  3.6 0.7 %copy-done.2 = s32[1,1,8]{2,1,0:T(1,128)S(1)} copy-done((s32[1,1,8]{2,1,0:T(1,128)S(1)}, s32[1,1,8]{2,1,0:T(1,128)}, u32[]{:S(2)}) %copy-start.2) | copy-done | bytes 56
  4.3 0.0 copy-start.3
  4.3 0.7 %copy-done.3 = s32[1,1,8]{2,1,0:T(1,128)S(1)} copy-done((s32[1,1,8]{2,1,0:T(1,128)S(1)}, s32[1,1,8]{2,1,0:T(1,128)}, u32[]{:S(2)}) %copy-start.3) | copy-done | bytes 56
  4.9 59.7 %shard_map.55 = f32[16,1024]{1,0:T(8,128)S(1)} custom-call(bf16[16,1024]{1,0:T(8,128)(2,1)S(1)} %copy-done.1, bf16[8,512,512]{2,1,0:T(8,128)(2,1)S(1)} %bitcast.5, s32[8]{0:T(128)S(1)} %bitcast.6, s32[8]{0:T(128)S(1)} %bitcast.7, s32[1]{0:T(128)} %bitcast.4.cnt), custom_call_target="tpu_custom_call" | custom-call | tf_op jit(solution)/shard_map/pallas_call | solution.py:328
  64.6 0.6 copy.8
Async XLA Ops:
  0.7 2.2 %copy-start = (bf16[1,1,8,512,512]{4,3,2,1,0:T(8,128)(2,1)S(1)}, bf16[1,1,8,512,512]{4,3,2,1,0:T(8,128)(2,1)}, u32[]{:S(2)}) copy-start(bf16[1,1,8,512,512]{4,3,2,1,0:T(8,128)(2,1)} %param.6) | copy-start | bytes 12582916
  2.8 0.8 %copy-start.1 = (bf16[16,1024]{1,0:T(8,128)(2,1)S(1)}, bf16[16,1024]{1,0:T(8,128)(2,1)}, u32[]{:S(2)}) copy-start(bf16[16,1024]{1,0:T(8,128)(2,1)} %vec.1) | copy-start | bytes 98308
  3.6 0.7 %copy-start.2 = (s32[1,1,8]{2,1,0:T(1,128)S(1)}, s32[1,1,8]{2,1,0:T(1,128)}, u32[]{:S(2)}) copy-start(s32[1,1,8]{2,1,0:T(1,128)} %param.7) | copy-start | bytes 100
  4.3 0.7 %copy-start.3 = (s32[1,1,8]{2,1,0:T(1,128)S(1)}, s32[1,1,8]{2,1,0:T(1,128)}, u32[]{:S(2)}) copy-start(s32[1,1,8]{2,1,0:T(1,128)} %param.8) | copy-start | bytes 100

commit v2 on v1

v2 whole, which is shorter than its diff:
```python
import jax
import jax.numpy as jnp
from jax import lax
from jax.experimental import pallas as pl
from jax.experimental.pallas import tpu as pltpu
from jax.sharding import PartitionSpec as P

NX, NH, NC = 4, 2, 2
NY, NZ = 4, 8
VECS, BLK, SLOTS = 16, 512, 8
LANES = 128
LT = BLK // LANES
EXPO = SLOTS * LT
MSG = EXPO + 1
MESH = pl.DeviceIdType.MESH
TINY = 2.0 ** -110


def exponent_of(most):
    return jnp.ceil(jnp.log2(jnp.maximum(most, TINY)) - 14.98)


def coded(values, inverse):
    return jnp.round(values * inverse).astype(jnp.int32).astype(jnp.int16)


def decoded(code):
    return code.astype(jnp.int32).astype(jnp.float32)


def most_of(parts):
    most = jnp.abs(parts[0])
    for part in parts[1:]:
        most = jnp.maximum(most, jnp.abs(part))
    return most


def kernel(
    vec, tiles, br_hbm, bc_hbm, cnt_hbm, out,
    br, bc, cnt, rto, cto, rprev, rlast, cprev, clast,
    rowbuf, colbuf, tilebuf, prod, ymsg, cmsg, run,
    zsend, zrecv, xsend, xrecv, hsend, hrecv, own,
    isem, vsem, tsem, ys, yr, zs, zr, cs, cr, ss, sr, ms, mr, ks, kr, ps, pr, xs, xr, hs, hr, js, jr,
):
    me_r, me_c = lax.axis_index("row"), lax.axis_index("col")
    x, h, core = me_r // (NH * NC), (me_r // NC) % NH, me_r % NC
    y, z = me_c // NZ, me_c % NZ

    def row_of(xx, hh, cc):
        return (xx * NH + hh) * NC + cc

    def col_of(yy, zz):
        return yy * NZ + zz

    def y_at(d):
        return (y + d + NY) % NY

    def z_at(d):
        return (z + d + NZ) % NZ

    def x_at(d):
        return (x + d + NX) % NX

    sibling = (row_of(x, h, 1 - core), me_c)
    far = (row_of(x, 1 - h, core), me_c)
    x_peer = [None] + [(row_of(x_at(d), h, core), me_c) for d in range(1, NX)]
    y_peer = [None] + [(me_r, col_of(y_at(d), z)) for d in range(1, NY)]
    z_peer = [None] + [(me_r, col_of(y, z_at(d))) for d in range(1, NZ)]

    def remote(src, dst, send, recv, device):
        return pltpu.make_async_remote_copy(
            src_ref=src, dst_ref=dst, send_sem=send, recv_sem=recv,
            device_id=device, device_id_type=MESH,
        )

    sent = []

    def send(*args):
        copy = remote(*args)
        copy.start()
        sent.append(copy)

    barrier = pltpu.get_barrier_semaphore()
    partners = [sibling, far] + x_peer[1:] + y_peer[1:] + z_peer[1:]
    for device in partners:
        pl.semaphore_signal(barrier, inc=1, device_id=device, device_id_type=MESH)

    into = []
    for k in range(2):
        piece = vec.at[:, pl.ds(k * BLK, BLK)]
        into.append(pltpu.make_async_copy(piece, rowbuf.at[2 * me_c + k], vsem.at[k]))
        into.append(pltpu.make_async_copy(piece, colbuf.at[2 * me_r + k], vsem.at[2 + k]))
    into.append(pltpu.make_async_copy(br_hbm.at[0, 0], br, isem.at[0]))
    into.append(pltpu.make_async_copy(bc_hbm.at[0, 0], bc, isem.at[1]))
    into.append(pltpu.make_async_copy(cnt_hbm.at[0], cnt, isem.at[2]))
    for copy in into:
        copy.start()
    for s in range(SLOTS):
        pltpu.make_async_copy(tiles.at[0, 0, s], tilebuf.at[s], tsem.at[s]).start()
    for copy in into:
        copy.wait()
    live = cnt[0]
    for s in range(SLOTS):
        rto[0, s] = jnp.where(s < live, br[s], -1)
        cto[0, s] = jnp.where(s < live, bc[s], -1)
    pl.semaphore_wait(barrier, len(partners))

    def row_chunk(dy, dz):
        return rowbuf.at[pl.ds(2 * col_of(y_at(-dy), z_at(-dz)), 2)]

    def col_chunk(d, e, cc):
        return colbuf.at[pl.ds(2 * row_of(x_at(-d), (h + e) % NH, cc), 2)]

    def relay(way, hop, i):
        chunk = row_chunk(i, way * hop)
        w = 0 if way > 0 else 1
        send(chunk, chunk, zs.at[w, hop, i], zr.at[w, hop, i], z_peer[way % NZ])

    def relay_wait(way, hop, i):
        chunk = row_chunk(i, way * (hop + 1))
        w = 0 if way > 0 else 1
        remote(chunk, chunk, zs.at[w, hop, i], zr.at[w, hop, i], z_peer[1]).wait_recv()

    def last_goes(way, i):
        return (i < NY // 2) == (way > 0)

    def col_wait(d, e):
        chunk = col_chunk(d, e, core)
        remote(chunk, chunk, cs.at[d, e], cr.at[d, e], far).wait_recv()

    def to_sibling(d, e):
        chunk = col_chunk(d, e, core)
        send(chunk, chunk, ss.at[d, e], sr.at[d, e], sibling)

    def tables(to, prev, last, sources, target_of):
        names = [to[n, s] for n in range(sources) for s in range(SLOTS)]
        for c, name in enumerate(names):
            found = jnp.int32(len(names))
            for earlier in range(c):
                found = jnp.where(names[earlier] == name, earlier, found)
            prev[c] = found
        for t in range(16):
            found = jnp.int32(len(names))
            for c, name in enumerate(names):
                found = jnp.where(name == target_of(t), c, found)
            last[t] = found

    mine_row, mine_col = row_chunk(0, 0), col_chunk(0, 0, core)
    send(mine_col, mine_col, cs.at[0, 1], cr.at[0, 1], far)
    for d in range(1, NY):
        send(mine_row, mine_row, ys.at[d], yr.at[d], y_peer[d])
    relay(1, 0, 0)
    relay(-1, 0, 0)
    for d in range(1, NX):
        send(mine_col, mine_col, cs.at[d, 0], cr.at[d, 0], x_peer[d])
    to_sibling(0, 0)
    send(cto.at[0], cto.at[1], js.at[0], jr.at[0], sibling)
    for d in range(1, NY):
        send(rto.at[0], rto.at[d], js.at[d], jr.at[d], y_peer[d])

    remote(cto.at[0], cto.at[1], js.at[0], jr.at[0], sibling).wait_recv()
    tables(cto, cprev, clast, NC, lambda t: (t // 2) * 2 * NC + 2 * core + t % 2)

    for i in range(1, NY):
        chunk = row_chunk(i, 0)
        remote(chunk, chunk, ys.at[i], yr.at[i], y_peer[1]).wait_recv()
        relay(1, 0, i)
        relay(-1, 0, i)
    for way in (1, -1):
        relay_wait(way, 0, 0)
        relay(way, 1, 0)

    for d in range(1, NY):
        remote(rto.at[0], rto.at[d], js.at[d], jr.at[d], y_peer[1]).wait_recv()
    tables(rto, rprev, rlast, NY, lambda t: 2 * col_of(y, 0) + t)

    col_wait(0, 1)
    theirs = col_chunk(0, 1, core)
    for d in range(1, NX):
        send(theirs, theirs, cs.at[d, 1], cr.at[d, 1], x_peer[d])
    to_sibling(0, 1)
    for d in range(1, NX):
        col_wait(d, 0)
        to_sibling(d, 0)

    for i in range(1, NY):
        for way in (1, -1):
            relay_wait(way, 0, i)
            relay(way, 1, i)
    for way in (1, -1):
        relay_wait(way, 1, 0)
        relay(way, 2, 0)

    for d in range(1, NX):
        col_wait(d, 1)
        to_sibling(d, 1)

    for i in range(1, NY):
        for way in (1, -1):
            relay_wait(way, 1, i)
            relay(way, 2, i)

    for e in range(NH):
        for d in range(NX):
            chunk = col_chunk(d, e, 1 - core)
            remote(chunk, chunk, ss.at[d, e], sr.at[d, e], sibling).wait_recv()

    def lane_parts(value):
        return [value[:, j * LANES:(j + 1) * LANES] for j in range(LT)]

    def products(pieces, where, contract, wait, msg):
        most = jnp.zeros((VECS, LANES), jnp.float32)
        for s in range(SLOTS):
            if wait:
                pltpu.make_async_copy(tiles.at[0, 0, s], tilebuf.at[s], tsem.at[s]).wait()
            value = lax.dot_general(
                pieces[where[s]], tilebuf[s], (((1,), (contract,)), ((), ())),
                preferred_element_type=jnp.float32,
            )
            value = jnp.where(s < live, value, 0.0)
            prod[s] = value
            most = jnp.maximum(most, most_of(lane_parts(value)))
        exponent = exponent_of(most)
        inverse = 1.0 / jnp.exp2(exponent)
        for s in range(SLOTS):
            for j, part in enumerate(lane_parts(prod[s])):
                msg[0, s * LT + j] = coded(part, inverse)
        msg[0, EXPO] = exponent.astype(jnp.int32).astype(jnp.int16)

    def combine(msg, sources, prev):
        run[sources * SLOTS] = jnp.zeros((LT, VECS, LANES), jnp.float32)
        for n in range(sources):
            scale = jnp.exp2(decoded(msg[n, EXPO]))

            def slot(s, carry):
                c = n * SLOTS + s
                before = run[prev[c]]
                for j in range(LT):
                    run[c, j] = decoded(msg[n, s * LT + j]) * scale + before[j]
                return carry

            lax.fori_loop(0, SLOTS, slot, 0)

    def block_parts(last, t):
        value = run[last[t]]
        return [value[j] for j in range(LT)]

    products(colbuf, bc, 1, True, ymsg)
    for d in range(1, NY):
        send(ymsg.at[0], ymsg.at[d], ps.at[d], pr.at[d], y_peer[d])

    for i in range(NY):
        for way in (1, -1):
            relay_wait(way, 2, i)
            if last_goes(way, i):
                relay(way, 3, i)
    for i in range(NY):
        relay_wait(1 if last_goes(1, i) else -1, 3, i)

    products(rowbuf, br, 0, False, cmsg)
    send(cmsg.at[0], cmsg.at[1], ms.at[0], mr.at[0], sibling)

    def code_chunk(parts, dst, first):
        exponent = exponent_of(most_of(parts))
        inverse = 1.0 / jnp.exp2(exponent)
        for t, part in enumerate(parts):
            dst[first + t] = coded(part, inverse)
        dst[first + len(parts)] = exponent.astype(jnp.int32).astype(jnp.int16)

    def chip_parts(xx, e):
        chip = xx * NH + (h + e) % NH
        return block_parts(clast, 2 * chip) + block_parts(clast, 2 * chip + 1)

    remote(cmsg.at[0], cmsg.at[1], ms.at[0], mr.at[0], sibling).wait_recv()
    combine(cmsg, NC, cprev)
    CH = 2 * LT + 1
    for d in range(1, NX):
        for e in range(NH):
            code_chunk(chip_parts(x_at(d), e), xsend.at[d], e * CH)
        send(xsend.at[d], xrecv.at[d], xs.at[d], xr.at[d], x_peer[d])
    for e in range(NH):
        for t, part in enumerate(chip_parts(x, e)):
            own[e, t] = part

    for d in range(1, NY):
        remote(ymsg.at[0], ymsg.at[d], ps.at[d], pr.at[d], y_peer[1]).wait_recv()
    combine(ymsg, NY, rprev)
    for d in range(1, NZ):
        to = z_at(d)
        code_chunk(block_parts(rlast, 2 * to) + block_parts(rlast, 2 * to + 1), zsend.at[d], 0)
        send(zsend.at[d], zrecv.at[d], ks.at[d], kr.at[d], z_peer[d])

    def opened(msg, first):
        scale = jnp.exp2(decoded(msg[first + 2 * LT]))
        return [decoded(msg[first + t]) * scale for t in range(2 * LT)]

    for d in range(1, NX):
        remote(xsend.at[d], xrecv.at[d], xs.at[d], xr.at[d], x_peer[1]).wait_recv()

    def with_x(e):
        parts = [own[e, t] for t in range(2 * LT)]
        for d in range(1, NX):
            parts = [a + b for a, b in zip(parts, opened(xrecv.at[d], e * CH))]
        return parts

    code_chunk(with_x(1), hsend, 0)
    send(hsend, hrecv, hs.at[0], hr.at[0], far)
    mine = block_parts(rlast, 2 * z) + block_parts(rlast, 2 * z + 1)
    total = [a + b for a, b in zip(with_x(0), mine)]
    for d in range(1, NZ):
        remote(zsend.at[d], zrecv.at[d], ks.at[d], kr.at[d], z_peer[1]).wait_recv()
        total = [a + b for a, b in zip(total, opened(zrecv.at[d], 0))]
    remote(hsend, hrecv, hs.at[0], hr.at[0], far).wait_recv()
    total = [a + b for a, b in zip(total, opened(hrecv, 0))]
    for t, part in enumerate(total):
        out[:, t * LANES:(t + 1) * LANES] = part

    for copy in sent:
        copy.wait_send()


def on_device(vectors, tiles, block_rows, block_cols, counts):
    i16, f32, bf16 = jnp.int16, jnp.float32, jnp.bfloat16
    chunk = 2 * LT + 1
    dma = pltpu.SemaphoreType.DMA

    def smem(shape):
        return pltpu.SMEM(shape, jnp.int32)

    scratch = [
        smem((SLOTS,)), smem((SLOTS,)), smem((1,)),
        smem((NY, SLOTS)), smem((NC, SLOTS)),
        smem((NY * SLOTS,)), smem((16,)),
        smem((NC * SLOTS,)), smem((16,)),
        pltpu.VMEM((2 * NY * NZ, VECS, BLK), bf16),
        pltpu.VMEM((2 * NX * NH * NC, VECS, BLK), bf16),
        pltpu.VMEM((SLOTS, BLK, BLK), bf16),
        pltpu.VMEM((SLOTS, VECS, BLK), f32),
        pltpu.VMEM((NY, MSG, VECS, LANES), i16),
        pltpu.VMEM((NC, MSG, VECS, LANES), i16),
        pltpu.VMEM((NY * SLOTS + 1, LT, VECS, LANES), f32),
        pltpu.VMEM((NZ, chunk, VECS, LANES), i16),
        pltpu.VMEM((NZ, chunk, VECS, LANES), i16),
        pltpu.VMEM((NX, NH * chunk, VECS, LANES), i16),
        pltpu.VMEM((NX, NH * chunk, VECS, LANES), i16),
        pltpu.VMEM((chunk, VECS, LANES), i16),
        pltpu.VMEM((chunk, VECS, LANES), i16),
        pltpu.VMEM((NH, 2 * LT, VECS, LANES), f32),
        dma((3,)), dma((4,)),
        dma((SLOTS,)),
        dma((NY,)), dma((NY,)),
        dma((2, NZ // 2, NY)), dma((2, NZ // 2, NY)),
        dma((NX, NH)), dma((NX, NH)),
        dma((NX, NH)), dma((NX, NH)),
        dma((1,)), dma((1,)),
        dma((NZ,)), dma((NZ,)),
        dma((NY,)), dma((NY,)),
        dma((NX,)), dma((NX,)),
        dma((1,)), dma((1,)),
        dma((NY,)), dma((NY,)),
    ]
    return pl.pallas_call(
        kernel,
        out_shape=jax.ShapeDtypeStruct((VECS, 2 * BLK), f32),
        in_specs=[pl.BlockSpec(memory_space=pltpu.HBM)] * 5,
        out_specs=pl.BlockSpec(memory_space=pltpu.VMEM),
        scratch_shapes=scratch,
        compiler_params=pltpu.CompilerParams(
            collective_id=0, has_side_effects=True, vmem_limit_bytes=64 * 2 ** 20
        ),
    )(vectors, tiles, block_rows, block_cols, counts)


def solution(mesh):
    placed = (
        P(None, ("row", "col")),
        P("row", "col", None, None, None),
        P("row", "col", None),
        P("row", "col", None),
        P("row", "col"),
    )
    return jax.shard_map(
        on_device, mesh=mesh, in_specs=placed, out_specs=P(None, ("row", "col")), check_vma=False
    )
```

time: 65.4 us -> 56.1 us (0.86)
  the two profiles are of different devices: /device:TPU:56 before, /device:TPU:8 now
where the time goes in v2:
time: 56.1 us; the launch traced here: 55.9 us
  Pallas kernels  53.7 us (96%)
  local copies, waits for them, and re-layouts  1.47 us (3%)
  between operations  0.66 us (1%)
    pallas_call x1, Pallas kernels, on_device(): pl.pallas_call(kernel, out_shape=jax.ShapeDtypeStruct((VECS, 2 * BLK), f3...  53.7 us
    unnamed x1, local copies, waits for them, and re-layouts  1.47 us

profile of v2, /device:TPU:8, one launch (start us, length us, event | category | flops | bytes accessed | tf_op | source)
XLA Modules:
  0.0 55.9 jit_solution(17277271691662905882)
XLA Ops:
  0.7 53.7 %shard_map.55 = f32[16,1024]{1,0:T(8,128)} custom-call(bf16[16,1024]{1,0:T(8,128)(2,1)} %vec.1, bf16[1,1,8,512,512]{4,3,2,1,0:T(8,128)(2,1)} %tiles.1, s32[1,1,8]{2,1,0:T(1,128)} %br_hbm.1, s32[1,1,8]{2,1,0:T(1,128)} %bc_hbm.1, s32[1,1]{1,0:T(1,128)S(6)} %copy.7.cnt_hbm), custom_call_target="tpu_custom_call" | custom-call | tf_op jit(solution)/shard_map/pallas_call | solution.py:362
  54.4 1.5 %copy.8 = f32[16,1024]{1,0:T(8,128)} copy(f32[16,1024]{1,0:T(8,128)} %shard_map.55) | data formatting | bytes 131072

commit v3 on v2

v3 whole, which is shorter than its diff:
```python
import jax
import jax.numpy as jnp
from jax import lax
from jax.experimental import pallas as pl
from jax.experimental.pallas import tpu as pltpu
from jax.sharding import PartitionSpec as P

NX, NH, NC = 4, 2, 2
NY, NZ = 4, 8
VECS, BLK, SLOTS = 16, 512, 8
SQ, PLACES = NY, NZ
WAYS = (1, -1)
LANES = 128
LT = BLK // LANES
HALF = SLOTS // 2
PART = HALF * LT + 1
MESH = pl.DeviceIdType.MESH
TINY = 2.0 ** -110


def exponent_of(most):
    return jnp.ceil(jnp.log2(jnp.maximum(most, TINY)) - 14.98)


def coded(values, inverse):
    return jnp.round(values * inverse).astype(jnp.int32).astype(jnp.int16)


def decoded(code):
    return code.astype(jnp.int32).astype(jnp.float32)


def most_of(parts):
    most = jnp.abs(parts[0])
    for part in parts[1:]:
        most = jnp.maximum(most, jnp.abs(part))
    return most


def kernel(
    vec, tiles, br_hbm, bc_hbm, cnt_hbm, out,
    br, bc, cnt, rto, cto, rprev, rlast, cprev, clast,
    rowbuf, colbuf, tilebuf, turned, ymsg, cmsg, run,
    zsend, zrecv, xsend, xrecv, hsend, hrecv, own,
    isem, vsem, tsem, ys, yr, zs, zr, qs, qr, us, ur, cs, cr, ss, sr, ms, mr, ks, kr, ps, pr, xs, xr, hs, hr, js, jr,
):
    me_r, me_c = lax.axis_index("row"), lax.axis_index("col")
    x, h, core = me_r // (NH * NC), (me_r // NC) % NH, me_r % NC
    y, z = me_c // NZ, me_c % NZ

    def row_of(xx, hh, cc):
        return (xx * NH + hh) * NC + cc

    def col_of(yy, zz):
        return yy * NZ + zz

    def y_at(d):
        return (y + d + NY) % NY

    def z_at(d):
        return (z + d + NZ) % NZ

    def x_at(d):
        return (x + d + NX) % NX

    sibling = (row_of(x, h, 1 - core), me_c)
    far = (row_of(x, 1 - h, core), me_c)
    x_peer = [None] + [(row_of(x_at(d), h, core), me_c) for d in range(1, NX)]
    y_peer = [None] + [(me_r, col_of(y_at(d), z)) for d in range(1, NY)]
    z_peer = [None] + [(me_r, col_of(y, z_at(d))) for d in range(1, NZ)]

    def remote(src, dst, send, recv, device):
        return pltpu.make_async_remote_copy(
            src_ref=src, dst_ref=dst, send_sem=send, recv_sem=recv,
            device_id=device, device_id_type=MESH,
        )

    sent = []

    def send(*args):
        copy = remote(*args)
        copy.start()
        sent.append(copy)

    barrier = pltpu.get_barrier_semaphore()
    partners = [sibling, far] + x_peer[1:] + y_peer[1:] + z_peer[1:]
    for device in partners:
        pl.semaphore_signal(barrier, inc=1, device_id=device, device_id_type=MESH)

    local = [
        pltpu.make_async_copy(br_hbm.at[0, 0], br, isem.at[0]),
        pltpu.make_async_copy(bc_hbm.at[0, 0], bc, isem.at[1]),
        pltpu.make_async_copy(cnt_hbm.at[0], cnt, isem.at[2]),
        pltpu.make_async_copy(vec, rowbuf.at[me_c], vsem.at[0]),
        pltpu.make_async_copy(vec, colbuf.at[me_r], vsem.at[1]),
    ]
    for copy in local:
        copy.start()
    pl.semaphore_wait(barrier, len(partners))

    def row_chunk(dy, dz):
        return rowbuf.at[col_of(y_at(-dy), z_at(-dz))]

    def col_chunk(d, e, cc):
        return colbuf.at[row_of(x_at(-d), (h + e) % NH, cc)]

    def pass_on(way, hop, i):
        chunk = row_chunk(i, way * hop)
        source = vec if hop == 0 and i == 0 else chunk
        w = WAYS.index(way)
        send(source, chunk, qs.at[w, hop, i], qr.at[w, hop, i], z_peer[way % NZ])

    def passed(way, hop, i):
        chunk = row_chunk(i, way * (hop + 1))
        w = WAYS.index(way)
        remote(chunk, chunk, qs.at[w, hop, i], qr.at[w, hop, i], z_peer[1]).wait_recv()

    def step(hop, group):
        for i in group:
            for way in WAYS:
                passed(way, hop, i)
                pass_on(way, hop + 1, i)

    def col_wait(d, e):
        chunk = col_chunk(d, e, core)
        remote(chunk, chunk, cs.at[d, e], cr.at[d, e], far).wait_recv()

    def to_sibling(d, e):
        chunk = col_chunk(d, e, core)
        source = vec if d == 0 and e == 0 else chunk
        send(source, chunk, ss.at[d, e], sr.at[d, e], sibling)

    def tables(to, prev, last, sources, target_of):
        names = [to[n, s] for n in range(sources) for s in range(SLOTS)]
        for c, name in enumerate(names):
            found = jnp.int32(len(names))
            for earlier in range(c):
                found = jnp.where(names[earlier] == name, earlier, found)
            prev[c] = found
        for t in range(16):
            found = jnp.int32(len(names))
            for c, name in enumerate(names):
                found = jnp.where(name == target_of(t), c, found)
            last[t] = found

    mine_row, mine_col = row_chunk(0, 0), col_chunk(0, 0, core)
    send(vec, mine_col, cs.at[0, 1], cr.at[0, 1], far)
    for d in range(1, NY):
        send(vec, mine_row, ys.at[d], yr.at[d], y_peer[d])
    for d in range(1, NX):
        send(vec, mine_col, cs.at[d, 0], cr.at[d, 0], x_peer[d])
    send(vec, mine_row, zs.at[0], zr.at[0], z_peer[NZ // 2])
    for way in WAYS:
        pass_on(way, 0, 0)
    to_sibling(0, 0)

    for s in range(SLOTS):
        pltpu.make_async_copy(tiles.at[0, 0, s], tilebuf.at[s], tsem.at[s]).start()
    for copy in local:
        copy.wait()
    live = cnt[0]
    for s in range(SLOTS):
        rto[0, s] = jnp.where(s < live, br[s], -1)
        cto[0, s] = jnp.where(s < live, bc[s], -1)
    send(cto.at[0], cto.at[1], js.at[0], jr.at[0], sibling)
    for d in range(1, SQ):
        send(rto.at[0], rto.at[d], js.at[d], jr.at[d], y_peer[d])

    for s in range(SLOTS):
        pltpu.make_async_copy(tiles.at[0, 0, s], tilebuf.at[s], tsem.at[s]).wait()

    def turn(s, carry):
        turned[s] = tilebuf[s].T
        return carry

    lax.fori_loop(0, SLOTS, turn, 0)

    for i in range(1, NY):
        chunk = row_chunk(i, 0)
        remote(chunk, chunk, ys.at[i], yr.at[i], y_peer[1]).wait_recv()
        for way in WAYS:
            pass_on(way, 0, i)
    step(0, [0])

    col_wait(0, 1)
    theirs = col_chunk(0, 1, core)
    for d in range(1, NX):
        send(theirs, theirs, cs.at[d, 1], cr.at[d, 1], x_peer[d])
    to_sibling(0, 1)

    chunk = row_chunk(0, NZ // 2)
    remote(chunk, chunk, zs.at[0], zr.at[0], z_peer[1]).wait_recv()
    for d in range(1, NY):
        send(chunk, chunk, us.at[d], ur.at[d], y_peer[d])

    for d in range(1, NX):
        col_wait(d, 0)
        to_sibling(d, 0)
    step(0, range(1, NY))
    step(1, [0])
    for d in range(1, NX):
        col_wait(d, 1)
        to_sibling(d, 1)
    for e in range(NH):
        for d in range(NX):
            chunk = col_chunk(d, e, 1 - core)
            remote(chunk, chunk, ss.at[d, e], sr.at[d, e], sibling).wait_recv()

    def lane_parts(value):
        return [value[:, j * LANES:(j + 1) * LANES] for j in range(LT)]

    def products(pieces, where, blocks, msg, part):
        values = []
        for s in range(part * HALF, (part + 1) * HALF):
            pair = pieces[where[s] // 2]
            piece = jnp.where(where[s] % 2 == 0, pair[:, :BLK], pair[:, BLK:])
            value = jnp.dot(piece, blocks[s], preferred_element_type=jnp.float32)
            values += lane_parts(jnp.where(s < live, value, 0.0))
        exponent = exponent_of(most_of(values))
        inverse = 1.0 / jnp.exp2(exponent)
        for t, value in enumerate(values):
            msg[0, part, t] = coded(value, inverse)
        msg[0, part, PART - 1] = exponent.astype(jnp.int32).astype(jnp.int16)

    def combine(msg, sources, prev):
        run[sources * SLOTS] = jnp.zeros((LT, VECS, LANES), jnp.float32)
        for n in range(sources):
            for part in range(2):
                scale = jnp.exp2(decoded(msg[n, part, PART - 1]))

                def slot(s, carry):
                    c = n * SLOTS + part * HALF + s
                    before = run[prev[c]]
                    for j in range(LT):
                        run[c, j] = decoded(msg[n, part, s * LT + j]) * scale + before[j]
                    return carry

                lax.fori_loop(0, HALF, slot, 0)

    def block_parts(last, t):
        value = run[last[t]]
        return [value[j] for j in range(LT)]

    for part in range(2):
        products(colbuf, bc, turned, ymsg, part)
        for d in range(1, SQ):
            send(ymsg.at[0, part], ymsg.at[d, part], ps.at[d, part], pr.at[d, part], y_peer[d])

    step(1, range(1, NY))
    remote(cto.at[0], cto.at[1], js.at[0], jr.at[0], sibling).wait_recv()
    tables(cto, cprev, clast, NC, lambda t: (t // 2) * 2 * NC + 2 * core + t % 2)
    for d in range(1, SQ):
        remote(rto.at[0], rto.at[d], js.at[d], jr.at[d], y_peer[1]).wait_recv()
    tables(
        rto, rprev, rlast, SQ,
        lambda t: 2 * col_of(y, 0) + t,
    )

    for i in range(1, NY):
        chunk = row_chunk(i, NZ // 2)
        remote(chunk, chunk, us.at[i], ur.at[i], y_peer[1]).wait_recv()
    for i in range(NY):
        for way in WAYS:
            passed(way, 2, i)

    for part in range(2):
        products(rowbuf, br, tilebuf, cmsg, part)
        send(cmsg.at[0, part], cmsg.at[1, part], ms.at[part], mr.at[part], sibling)

    def code_chunk(parts, dst, first):
        exponent = exponent_of(most_of(parts))
        inverse = 1.0 / jnp.exp2(exponent)
        for t, part in enumerate(parts):
            dst[first + t] = coded(part, inverse)
        dst[first + len(parts)] = exponent.astype(jnp.int32).astype(jnp.int16)

    def chip_parts(xx, e):
        chip = xx * NH + (h + e) % NH
        return block_parts(clast, 2 * chip) + block_parts(clast, 2 * chip + 1)

    for part in range(2):
        remote(cmsg.at[0, part], cmsg.at[1, part], ms.at[part], mr.at[part], sibling).wait_recv()
    combine(cmsg, NC, cprev)
    CH = 2 * LT + 1
    for d in range(1, NX):
        for e in range(NH):
            code_chunk(chip_parts(x_at(d), e), xsend.at[d], e * CH)
        send(xsend.at[d], xrecv.at[d], xs.at[d], xr.at[d], x_peer[d])
    for e in range(NH):
        for t, part in enumerate(chip_parts(x, e)):
            own[e, t] = part

    def place_parts(q):
        first = 2 * z_at(q)
        return block_parts(rlast, first) + block_parts(rlast, first + 1)

    for d in range(1, SQ):
        for part in range(2):
            remote(ymsg.at[0, part], ymsg.at[d, part], ps.at[d, part], pr.at[d, part], y_peer[1]).wait_recv()
    combine(ymsg, SQ, rprev)
    for q in range(1, PLACES):
        code_chunk(place_parts(q), zsend.at[q], 0)
        send(zsend.at[q], zrecv.at[q], ks.at[q], kr.at[q], z_peer[q])

    def opened(msg, first):
        scale = jnp.exp2(decoded(msg[first + 2 * LT]))
        return [decoded(msg[first + t]) * scale for t in range(2 * LT)]

    for d in range(1, NX):
        remote(xsend.at[d], xrecv.at[d], xs.at[d], xr.at[d], x_peer[1]).wait_recv()

    def with_x(e):
        parts = [own[e, t] for t in range(2 * LT)]
        for d in range(1, NX):
            parts = [a + b for a, b in zip(parts, opened(xrecv.at[d], e * CH))]
        return parts

    code_chunk(with_x(1), hsend, 0)
    send(hsend, hrecv, hs.at[0], hr.at[0], far)
    total = [a + b for a, b in zip(with_x(0), place_parts(0))]
    for q in range(1, PLACES):
        remote(zsend.at[q], zrecv.at[q], ks.at[q], kr.at[q], z_peer[1]).wait_recv()
        total = [a + b for a, b in zip(total, opened(zrecv.at[q], 0))]
    remote(hsend, hrecv, hs.at[0], hr.at[0], far).wait_recv()
    total = [a + b for a, b in zip(total, opened(hrecv, 0))]
    for t, part in enumerate(total):
        out[:, t * LANES:(t + 1) * LANES] = part

    for copy in sent:
        copy.wait_send()


def on_device(vectors, tiles, block_rows, block_cols, counts):
    i16, f32, bf16 = jnp.int16, jnp.float32, jnp.bfloat16
    chunk = 2 * LT + 1
    dma = pltpu.SemaphoreType.DMA

    def smem(shape):
        return pltpu.SMEM(shape, jnp.int32)

    scratch = [
        smem((SLOTS,)), smem((SLOTS,)), smem((1,)),
        smem((SQ, SLOTS)), smem((NC, SLOTS)),
        smem((SQ * SLOTS,)), smem((16,)),
        smem((NC * SLOTS,)), smem((16,)),
        pltpu.VMEM((NY * NZ, VECS, 2 * BLK), bf16),
        pltpu.VMEM((NX * NH * NC, VECS, 2 * BLK), bf16),
        pltpu.VMEM((SLOTS, BLK, BLK), bf16),
        pltpu.VMEM((SLOTS, BLK, BLK), bf16),
        pltpu.VMEM((SQ, 2, PART, VECS, LANES), i16),
        pltpu.VMEM((NC, 2, PART, VECS, LANES), i16),
        pltpu.VMEM((SQ * SLOTS + 1, LT, VECS, LANES), f32),
        pltpu.VMEM((PLACES, chunk, VECS, LANES), i16),
        pltpu.VMEM((PLACES, chunk, VECS, LANES), i16),
        pltpu.VMEM((NX, NH * chunk, VECS, LANES), i16),
        pltpu.VMEM((NX, NH * chunk, VECS, LANES), i16),
        pltpu.VMEM((chunk, VECS, LANES), i16),
        pltpu.VMEM((chunk, VECS, LANES), i16),
        pltpu.VMEM((NH, 2 * LT, VECS, LANES), f32),
        dma((3,)), dma((2,)),
        dma((SLOTS,)),
        dma((NY,)), dma((NY,)),
        dma((1,)), dma((1,)),
        dma((2, NZ // 2 - 1, NY)), dma((2, NZ // 2 - 1, NY)),
        dma((NY,)), dma((NY,)),
        dma((NX, NH)), dma((NX, NH)),
        dma((NX, NH)), dma((NX, NH)),
        dma((2,)), dma((2,)),
        dma((PLACES,)), dma((PLACES,)),
        dma((SQ, 2)), dma((SQ, 2)),
        dma((NX,)), dma((NX,)),
        dma((1,)), dma((1,)),
        dma((SQ,)), dma((SQ,)),
    ]
    return pl.pallas_call(
        kernel,
        out_shape=jax.ShapeDtypeStruct((VECS, 2 * BLK), f32),
        in_specs=[pl.BlockSpec(memory_space=pltpu.HBM)] * 5,
        out_specs=pl.BlockSpec(memory_space=pltpu.VMEM),
        scratch_shapes=scratch,
        compiler_params=pltpu.CompilerParams(
            collective_id=0, has_side_effects=True, vmem_limit_bytes=64 * 2 ** 20
        ),
    )(vectors, tiles, block_rows, block_cols, counts)


def solution(mesh):
    placed = (
        P(None, ("row", "col")),
        P("row", "col", None, None, None),
        P("row", "col", None),
        P("row", "col", None),
        P("row", "col"),
    )
    return jax.shard_map(
        on_device, mesh=mesh, in_specs=placed, out_specs=P(None, ("row", "col")), check_vma=False
    )
```

time: 56.1 us -> 51.9 us (0.925)
  the two profiles are of different devices: /device:TPU:8 before, /device:TPU:1 now
where the time goes in v3:
time: 51.9 us; the launch traced here: 51.7 us
  Pallas kernels  49.6 us (96%)
  local copies, waits for them, and re-layouts  1.47 us (3%)
  between operations  0.66 us (1%)
    pallas_call x1, Pallas kernels, on_device(): pl.pallas_call(kernel, out_shape=jax.ShapeDtypeStruct((VECS, 2 * BLK), f3...  49.6 us
    unnamed x1, local copies, waits for them, and re-layouts  1.47 us

profile of v3, /device:TPU:1, one launch (start us, length us, event | category | flops | bytes accessed | tf_op | source)
XLA Modules:
  0.0 51.7 jit_solution(16564500051838551724)
XLA Ops:
  0.7 49.6 %shard_map.55 = f32[16,1024]{1,0:T(8,128)} custom-call(bf16[16,1024]{1,0:T(8,128)(2,1)} %vec.1, bf16[1,1,8,512,512]{4,3,2,1,0:T(8,128)(2,1)} %tiles.1, s32[1,1,8]{2,1,0:T(1,128)} %br_hbm.1, s32[1,1,8]{2,1,0:T(1,128)} %bc_hbm.1, s32[1,1]{1,0:T(1,128)S(6)} %copy.7.cnt_hbm), custom_call_target="tpu_custom_call" | custom-call | tf_op jit(solution)/shard_map/pallas_call | solution.py:375
  50.3 1.5 %copy.8 = f32[16,1024]{1,0:T(8,128)} copy(f32[16,1024]{1,0:T(8,128)} %shard_map.55) | data formatting | bytes 131072

commit v4 on v3

--- a/solution.py
+++ b/solution.py
@@ -14,6 +14,7 @@
 LT = BLK // LANES
 HALF = SLOTS // 2
 PART = HALF * LT + 1
+LONE = LT + 1
 MESH = pl.DeviceIdType.MESH
 TINY = 2.0 ** -110
 
@@ -40,9 +41,9 @@
 def kernel(
     vec, tiles, br_hbm, bc_hbm, cnt_hbm, out,
     br, bc, cnt, rto, cto, rprev, rlast, cprev, clast,
-    rowbuf, colbuf, tilebuf, turned, ymsg, cmsg, run,
+    rowbuf, colbuf, tilebuf, turned, ymsg, cmsg, lone, lent, kept, run,
     zsend, zrecv, xsend, xrecv, hsend, hrecv, own,
-    isem, vsem, tsem, ys, yr, zs, zr, qs, qr, us, ur, cs, cr, ss, sr, ms, mr, ks, kr, ps, pr, xs, xr, hs, hr, js, jr,
+    isem, vsem, tsem, ys, yr, zs, zr, qs, qr, us, ur, cs, cr, ss, sr, ms, mr, ks, kr, ps, pr, xs, xr, hs, hr, js, jr, es, er, fs, fr,
 ):
     me_r, me_c = lax.axis_index("row"), lax.axis_index("col")
     x, h, core = me_r // (NH * NC), (me_r // NC) % NH, me_r % NC
@@ -130,8 +131,7 @@
         source = vec if d == 0 and e == 0 else chunk
         send(source, chunk, ss.at[d, e], sr.at[d, e], sibling)
 
-    def tables(to, prev, last, sources, target_of):
-        names = [to[n, s] for n in range(sources) for s in range(SLOTS)]
+    def tables(names, prev, last, target_of):
         for c, name in enumerate(names):
             found = jnp.int32(len(names))
             for earlier in range(c):
@@ -209,52 +209,67 @@
     def lane_parts(value):
         return [value[:, j * LANES:(j + 1) * LANES] for j in range(LT)]
 
+    def product(pieces, where, blocks, s):
+        pair = pieces[where[s] // 2]
+        piece = jnp.where(where[s] % 2 == 0, pair[:, :BLK], pair[:, BLK:])
+        value = jnp.dot(piece, blocks[s], preferred_element_type=jnp.float32)
+        return lane_parts(jnp.where(s < live, value, 0.0))
+
+    def code_chunk(parts, dst, first):
+        exponent = exponent_of(most_of(parts))
+        inverse = 1.0 / jnp.exp2(exponent)
+        for t, part in enumerate(parts):
+            dst[first + t] = coded(part, inverse)
+        dst[first + len(parts)] = exponent.astype(jnp.int32).astype(jnp.int16)
+
     def products(pieces, where, blocks, msg, part):
         values = []
         for s in range(part * HALF, (part + 1) * HALF):
-            pair = pieces[where[s] // 2]
-            piece = jnp.where(where[s] % 2 == 0, pair[:, :BLK], pair[:, BLK:])
-            value = jnp.dot(piece, blocks[s], preferred_element_type=jnp.float32)
-            values += lane_parts(jnp.where(s < live, value, 0.0))
-        exponent = exponent_of(most_of(values))
-        inverse = 1.0 / jnp.exp2(exponent)
-        for t, value in enumerate(values):
-            msg[0, part, t] = coded(value, inverse)
-        msg[0, part, PART - 1] = exponent.astype(jnp.int32).astype(jnp.int16)
-
-    def combine(msg, sources, prev):
-        run[sources * SLOTS] = jnp.zeros((LT, VECS, LANES), jnp.float32)
-        for n in range(sources):
-            for part in range(2):
-                scale = jnp.exp2(decoded(msg[n, part, PART - 1]))
-
-                def slot(s, carry):
-                    c = n * SLOTS + part * HALF + s
-                    before = run[prev[c]]
-                    for j in range(LT):
-                        run[c, j] = decoded(msg[n, part, s * LT + j]) * scale + before[j]
-                    return carry
-
-                lax.fori_loop(0, HALF, slot, 0)
+            values += product(pieces, where, blocks, s)
+        code_chunk(values, msg, 0)
+
+    def combine(groups, prev):
+        count = sum(slots for _, slots in groups)
+        run[count] = jnp.zeros((LT, VECS, LANES), jnp.float32)
+        base = 0
+        for msg, slots in groups:
+            scale = jnp.exp2(decoded(msg[slots * LT]))
+            for s in range(slots):
+                before = run[prev[base + s]]
+                for j in range(LT):
+                    run[base + s, j] = decoded(msg[s * LT + j]) * scale + before[j]
+            base += slots
 
     def block_parts(last, t):
         value = run[last[t]]
         return [value[j] for j in range(LT)]
 
-    for part in range(2):
-        products(colbuf, bc, turned, ymsg, part)
-        for d in range(1, SQ):
-            send(ymsg.at[0, part], ymsg.at[d, part], ps.at[d, part], pr.at[d, part], y_peer[d])
+    for d in range(1, NY):
+        code_chunk(product(colbuf, bc, turned, HALF + d), lone.at[d], 0)
+        send(lone.at[d], lent.at[d], es.at[d], er.at[d], y_peer[d])
+    products(colbuf, bc, turned, ymsg.at[0], 0)
+    for d in range(1, SQ):
+        send(ymsg.at[0], ymsg.at[d], ps.at[d], pr.at[d], y_peer[d])
+    code_chunk(product(colbuf, bc, turned, HALF), lent.at[0], 0)
 
     step(1, range(1, NY))
-    remote(cto.at[0], cto.at[1], js.at[0], jr.at[0], sibling).wait_recv()
-    tables(cto, cprev, clast, NC, lambda t: (t // 2) * 2 * NC + 2 * core + t % 2)
     for d in range(1, SQ):
         remote(rto.at[0], rto.at[d], js.at[d], jr.at[d], y_peer[1]).wait_recv()
-    tables(
-        rto, rprev, rlast, SQ,
-        lambda t: 2 * col_of(y, 0) + t,
-    )
+    full = jnp.int32(0)
+    for n in range(1, SQ):
+        full = jnp.where(rto[n, HALF] >= 0, n, full)
+    for d in range(1, NY):
+        remote(lone.at[d], lent.at[d], es.at[d], er.at[d], y_peer[1]).wait_recv()
+    kept[0] = lent[full]
+    for d in range(1, NY):
+        send(kept.at[0], kept.at[d], fs.at[d], fr.at[d], y_peer[d])
+
+    remote(cto.at[0], cto.at[1], js.at[0], jr.at[0], sibling).wait_recv()
+    names = [cto[n, s] for n in range(NC) for s in range(SLOTS)]
+    tables(names, cprev, clast, lambda t: (t // 2) * 2 * NC + 2 * core + t % 2)
+    names = [rto[n, s] for n in range(SQ) for s in range(HALF)]
+    names += [rto[full, HALF + (full - m + NY) % NY] for m in range(NY)]
+    tables(names, rprev, rlast, lambda t: 2 * col_of(y, 0) + t)
 
     for i in range(1, NY):
         chunk = row_chunk(i, NZ // 2)
@@ -264,15 +279,8 @@
             passed(way, 2, i)
 
     for part in range(2):
-        products(rowbuf, br, tilebuf, cmsg, part)
+        products(rowbuf, br, tilebuf, cmsg.at[0, part], part)
         send(cmsg.at[0, part], cmsg.at[1, part], ms.at[part], mr.at[part], sibling)
-
-    def code_chunk(parts, dst, first):
-        exponent = exponent_of(most_of(parts))
-        inverse = 1.0 / jnp.exp2(exponent)
-        for t, part in enumerate(parts):
-            dst[first + t] = coded(part, inverse)
-        dst[first + len(parts)] = exponent.astype(jnp.int32).astype(jnp.int16)
 
     def chip_parts(xx, e):
         chip = xx * NH + (h + e) % NH
@@ -280,7 +288,7 @@
 
     for part in range(2):
         remote(cmsg.at[0, part], cmsg.at[1, part], ms.at[part], mr.at[part], sibling).wait_recv()
-    combine(cmsg, NC, cprev)
+    combine([(cmsg.at[n, part], HALF) for n in range(NC) for part in range(2)], cprev)
     CH = 2 * LT + 1
     for d in range(1, NX):
         for e in range(NH):
@@ -295,9 +303,9 @@
         return block_parts(rlast, first) + block_parts(rlast, first + 1)
 
     for d in range(1, SQ):
-        for part in range(2):
-            remote(ymsg.at[0, part], ymsg.at[d, part], ps.at[d, part], pr.at[d, part], y_peer[1]).wait_recv()
-    combine(ymsg, SQ, rprev)
+        remote(ymsg.at[0], ymsg.at[d], ps.at[d], pr.at[d], y_peer[1]).wait_recv()
+        remote(kept.at[0], kept.at[d], fs.at[d], fr.at[d], y_peer[1]).wait_recv()
+    combine([(ymsg.at[n], HALF) for n in range(SQ)] + [(kept.at[m], 1) for m in range(NY)], rprev)
     for q in range(1, PLACES):
         code_chunk(place_parts(q), zsend.at[q], 0)
         send(zsend.at[q], zrecv.at[q], ks.at[q], kr.at[q], z_peer[q])
@@ -341,15 +349,18 @@
     scratch = [
         smem((SLOTS,)), smem((SLOTS,)), smem((1,)),
         smem((SQ, SLOTS)), smem((NC, SLOTS)),
-        smem((SQ * SLOTS,)), smem((16,)),
+        smem((SQ * HALF + NY,)), smem((16,)),
         smem((NC * SLOTS,)), smem((16,)),
         pltpu.VMEM((NY * NZ, VECS, 2 * BLK), bf16),
         pltpu.VMEM((NX * NH * NC, VECS, 2 * BLK), bf16),
         pltpu.VMEM((SLOTS, BLK, BLK), bf16),
         pltpu.VMEM((SLOTS, BLK, BLK), bf16),
-        pltpu.VMEM((SQ, 2, PART, VECS, LANES), i16),
+        pltpu.VMEM((SQ, PART, VECS, LANES), i16),
         pltpu.VMEM((NC, 2, PART, VECS, LANES), i16),
-        pltpu.VMEM((SQ * SLOTS + 1, LT, VECS, LANES), f32),
+        pltpu.VMEM((NY, LONE, VECS, LANES), i16),
+        pltpu.VMEM((NY, LONE, VECS, LANES), i16),
+        pltpu.VMEM((NY, LONE, VECS, LANES), i16),
+        pltpu.VMEM((SQ * HALF + NY + 1, LT, VECS, LANES), f32),
         pltpu.VMEM((PLACES, chunk, VECS, LANES), i16),
         pltpu.VMEM((PLACES, chunk, VECS, LANES), i16),
         pltpu.VMEM((NX, NH * chunk, VECS, LANES), i16),
@@ -367,10 +378,12 @@
         dma((NX, NH)), dma((NX, NH)),
         dma((2,)), dma((2,)),
         dma((PLACES,)), dma((PLACES,)),
-        dma((SQ, 2)), dma((SQ, 2)),
+        dma((SQ,)), dma((SQ,)),
         dma((NX,)), dma((NX,)),
         dma((1,)), dma((1,)),
         dma((SQ,)), dma((SQ,)),
+        dma((NY,)), dma((NY,)),
+        dma((NY,)), dma((NY,)),
     ]
     return pl.pallas_call(
         kernel,

time: 51.9 us -> 51 us (0.983)
  Pallas kernels: 49.6 us -> 48.6 us
    pallas_call x1, Pallas kernels: 49.6 us -> 48.6 us  [on_device(): pl.pallas_call(kernel, out_shape=jax.ShapeDtypeStruct((VECS, 2 * BLK), f3...]
where the time goes in v4:
time: 51 us; the launch traced here: 50.8 us
  Pallas kernels  48.6 us (95%)
  local copies, waits for them, and re-layouts  1.47 us (3%)
  between operations  0.66 us (1%)
    pallas_call x1, Pallas kernels, on_device(): pl.pallas_call(kernel, out_shape=jax.ShapeDtypeStruct((VECS, 2 * BLK), f3...  48.6 us
    unnamed x1, local copies, waits for them, and re-layouts  1.47 us

profile of v4, /device:TPU:1, one launch (start us, length us, event | category | flops | bytes accessed | tf_op | source)
XLA Modules:
  0.0 50.8 jit_solution(11538307036264802126)
XLA Ops:
  0.7 48.6 %shard_map.55 = f32[16,1024]{1,0:T(8,128)} custom-call(bf16[16,1024]{1,0:T(8,128)(2,1)} %vec.1, bf16[1,1,8,512,512]{4,3,2,1,0:T(8,128)(2,1)} %tiles.1, s32[1,1,8]{2,1,0:T(1,128)} %br_hbm.1, s32[1,1,8]{2,1,0:T(1,128)} %bc_hbm.1, s32[1,1]{1,0:T(1,128)S(6)} %copy.7.cnt_hbm), custom_call_target="tpu_custom_call" | custom-call | tf_op jit(solution)/shard_map/pallas_call | solution.py:388
  49.3 1.5 %copy.8 = f32[16,1024]{1,0:T(8,128)} copy(f32[16,1024]{1,0:T(8,128)} %shard_map.55) | data formatting | bytes 131072

commit v5 on v4

--- a/solution.py
+++ b/solution.py
@@ -84,7 +84,7 @@
         sent.append(copy)
 
     barrier = pltpu.get_barrier_semaphore()
-    partners = [sibling, far] + x_peer[1:] + y_peer[1:] + z_peer[1:]
+    partners = [sibling, far] + x_peer[1:] + y_peer[1:] + [z_peer[1], z_peer[4], z_peer[7]]
     for device in partners:
         pl.semaphore_signal(barrier, inc=1, device_id=device, device_id_type=MESH)
 
@@ -105,6 +105,9 @@
     def col_chunk(d, e, cc):
         return colbuf.at[row_of(x_at(-d), (h + e) % NH, cc)]
 
+    def col_piece(ref, e, k):
+        return ref.at[:, pl.ds(k * BLK, BLK)] if e else ref
+
     def pass_on(way, hop, i):
         chunk = row_chunk(i, way * hop)
         source = vec if hop == 0 and i == 0 else chunk
@@ -122,14 +125,14 @@
                 passed(way, hop, i)
                 pass_on(way, hop + 1, i)
 
-    def col_wait(d, e):
-        chunk = col_chunk(d, e, core)
-        remote(chunk, chunk, cs.at[d, e], cr.at[d, e], far).wait_recv()
-
-    def to_sibling(d, e):
-        chunk = col_chunk(d, e, core)
+    def col_wait(d, e, k):
+        chunk = col_piece(col_chunk(d, e, core), e, k)
+        remote(chunk, chunk, cs.at[d, e, k], cr.at[d, e, k], far).wait_recv()
+
+    def to_sibling(d, e, k):
+        chunk = col_piece(col_chunk(d, e, core), e, k)
         source = vec if d == 0 and e == 0 else chunk
-        send(source, chunk, ss.at[d, e], sr.at[d, e], sibling)
+        send(source, chunk, ss.at[d, e, k], sr.at[d, e, k], sibling)
 
     def tables(names, prev, last, target_of):
         for c, name in enumerate(names):
@@ -144,15 +147,16 @@
             last[t] = found
 
     mine_row, mine_col = row_chunk(0, 0), col_chunk(0, 0, core)
-    send(vec, mine_col, cs.at[0, 1], cr.at[0, 1], far)
+    for k in range(2):
+        send(col_piece(vec, 1, k), col_piece(mine_col, 1, k), cs.at[0, 1, k], cr.at[0, 1, k], far)
     for d in range(1, NY):
         send(vec, mine_row, ys.at[d], yr.at[d], y_peer[d])
     for d in range(1, NX):
-        send(vec, mine_col, cs.at[d, 0], cr.at[d, 0], x_peer[d])
+        send(vec, mine_col, cs.at[d, 0, 0], cr.at[d, 0, 0], x_peer[d])
     send(vec, mine_row, zs.at[0], zr.at[0], z_peer[NZ // 2])
     for way in WAYS:
         pass_on(way, 0, 0)
-    to_sibling(0, 0)
+    to_sibling(0, 0, 0)
 
     for s in range(SLOTS):
         pltpu.make_async_copy(tiles.at[0, 0, s], tilebuf.at[s], tsem.at[s]).start()
@@ -182,11 +186,12 @@
             pass_on(way, 0, i)
     step(0, [0])
 
-    col_wait(0, 1)
-    theirs = col_chunk(0, 1, core)
-    for d in range(1, NX):
-        send(theirs, theirs, cs.at[d, 1], cr.at[d, 1], x_peer[d])
-    to_sibling(0, 1)
+    for k in range(2):
+        col_wait(0, 1, k)
+        theirs = col_piece(col_chunk(0, 1, core), 1, k)
+        for d in range(1, NX):
+            send(theirs, theirs, cs.at[d, 1, k], cr.at[d, 1, k], x_peer[d])
+        to_sibling(0, 1, k)
 
     chunk = row_chunk(0, NZ // 2)
     remote(chunk, chunk, zs.at[0], zr.at[0], z_peer[1]).wait_recv()
@@ -194,17 +199,19 @@
         send(chunk, chunk, us.at[d], ur.at[d], y_peer[d])
 
     for d in range(1, NX):
-        col_wait(d, 0)
-        to_sibling(d, 0)
+        col_wait(d, 0, 0)
+        to_sibling(d, 0, 0)
     step(0, range(1, NY))
     step(1, [0])
-    for d in range(1, NX):
-        col_wait(d, 1)
-        to_sibling(d, 1)
+    for k in range(2):
+        for d in range(1, NX):
+            col_wait(d, 1, k)
+            to_sibling(d, 1, k)
     for e in range(NH):
         for d in range(NX):
-            chunk = col_chunk(d, e, 1 - core)
-            remote(chunk, chunk, ss.at[d, e], sr.at[d, e], sibling).wait_recv()
+            for k in range(1 + e):
+                chunk = col_piece(col_chunk(d, e, 1 - core), e, k)
+                remote(chunk, chunk, ss.at[d, e, k], sr.at[d, e, k], sibling).wait_recv()
 
     def lane_parts(value):
         return [value[:, j * LANES:(j + 1) * LANES] for j in range(LT)]
@@ -228,10 +235,9 @@
             values += product(pieces, where, blocks, s)
         code_chunk(values, msg, 0)
 
-    def combine(groups, prev):
-        count = sum(slots for _, slots in groups)
-        run[count] = jnp.zeros((LT, VECS, LANES), jnp.float32)
-        base = 0
+    def combine(groups, prev, base, count):
+        if base == 0:
+            run[count] = jnp.zeros((LT, VECS, LANES), jnp.float32)
         for msg, slots in groups:
             scale = jnp.exp2(decoded(msg[slots * LT]))
             for s in range(slots):
@@ -288,7 +294,7 @@
 
     for part in range(2):
         remote(cmsg.at[0, part], cmsg.at[1, part], ms.at[part], mr.at[part], sibling).wait_recv()
-    combine([(cmsg.at[n, part], HALF) for n in range(NC) for part in range(2)], cprev)
+    combine([(cmsg.at[n, part], HALF) for n in range(NC) for part in range(2)], cprev, 0, NC * SLOTS)
     CH = 2 * LT + 1
     for d in range(1, NX):
         for e in range(NH):
@@ -302,10 +308,13 @@
         first = 2 * z_at(q)
         return block_parts(rlast, first) + block_parts(rlast, first + 1)
 
+    count = SQ * HALF + NY
     for d in range(1, SQ):
         remote(ymsg.at[0], ymsg.at[d], ps.at[d], pr.at[d], y_peer[1]).wait_recv()
+    combine([(ymsg.at[n], HALF) for n in range(SQ)], rprev, 0, count)
+    for d in range(1, NY):
         remote(kept.at[0], kept.at[d], fs.at[d], fr.at[d], y_peer[1]).wait_recv()
-    combine([(ymsg.at[n], HALF) for n in range(SQ)] + [(kept.at[m], 1) for m in range(NY)], rprev)
+    combine([(kept.at[m], 1) for m in range(NY)], rprev, SQ * HALF, count)
     for q in range(1, PLACES):
         code_chunk(place_parts(q), zsend.at[q], 0)
         send(zsend.at[q], zrecv.at[q], ks.at[q], kr.at[q], z_peer[q])
@@ -374,8 +383,8 @@
         dma((1,)), dma((1,)),
         dma((2, NZ // 2 - 1, NY)), dma((2, NZ // 2 - 1, NY)),
         dma((NY,)), dma((NY,)),
-        dma((NX, NH)), dma((NX, NH)),
-        dma((NX, NH)), dma((NX, NH)),
+        dma((NX, NH, 2)), dma((NX, NH, 2)),
+        dma((NX, NH, 2)), dma((NX, NH, 2)),
         dma((2,)), dma((2,)),
         dma((PLACES,)), dma((PLACES,)),
         dma((SQ,)), dma((SQ,)),

time: 51 us -> 50.4 us (0.988)
    pallas_call x1, Pallas kernels: 48.6 us -> 48.1 us  [on_device(): pl.pallas_call(kernel, out_shape=jax.ShapeDtypeStruct((VECS, 2 * BLK), f3...]
where the time goes in v5:
time: 50.4 us; the launch traced here: 50.2 us
  Pallas kernels  48.1 us (95%)
  local copies, waits for them, and re-layouts  1.47 us (3%)
  between operations  0.66 us (1%)
    pallas_call x1, Pallas kernels, on_device(): pl.pallas_call(kernel, out_shape=jax.ShapeDtypeStruct((VECS, 2 * BLK), f3...  48.1 us
    unnamed x1, local copies, waits for them, and re-layouts  1.47 us

profile of v5, /device:TPU:1, one launch (start us, length us, event | category | flops | bytes accessed | tf_op | source)
XLA Modules:
  0.0 50.2 jit_solution(13419219767283039596)
XLA Ops:
  0.7 48.1 %shard_map.55 = f32[16,1024]{1,0:T(8,128)} custom-call(bf16[16,1024]{1,0:T(8,128)(2,1)} %vec.1, bf16[1,1,8,512,512]{4,3,2,1,0:T(8,128)(2,1)} %tiles.1, s32[1,1,8]{2,1,0:T(1,128)} %br_hbm.1, s32[1,1,8]{2,1,0:T(1,128)} %bc_hbm.1, s32[1,1]{1,0:T(1,128)S(6)} %copy.7.cnt_hbm), custom_call_target="tpu_custom_call" | custom-call | tf_op jit(solution)/shard_map/pallas_call | solution.py:397
  48.7 1.5 %copy.8 = f32[16,1024]{1,0:T(8,128)} copy(f32[16,1024]{1,0:T(8,128)} %shard_map.55) | data formatting | bytes 131072
